TPU v7x, 512 devices: a whole 4x8x8 slice. The times are simulated.
512 devices in a mesh: video: 64 (over y_hi, x, z), mp: 8 (over y_lo, core).
Axes of the slice: x: 4, y: 8 (y_hi: 2, y_lo: 4; y = y_hi * 4 + y_lo), z: 8, core: 2. Of those that a mesh axis runs over, the one named last changes fastest.
Arguments:
- frames: bfloat16 [16384, 4096], P('video', 'mp'), may hold values from -36 to 36
- cotangent: bfloat16 [192, 128, 4096], P('video'), may hold values from -6 to 6
- w_qkv: bfloat16 [4096, 16, 384], P('video', 'mp'), as said below
- w_out: bfloat16 [128, 16, 4096], P('video', 'mp'), may hold values from -0.125 to 0.125
- starts: int32 [192], P('video'), may hold values from 0 to 255, as said below
- counts: int32 [64], P('video'), may hold values from 0 to 3
Outputs:
- frame_grads: float32 [16384, 4096], P('video', 'mp')
Inputs may be any that keep to these rules, and one draw needn't show every extreme that they name: Windows lie inside the video: a slot of the last shard starts at most 128; slots of other shards may reach into the next shard; slots at or beyond their shard's count are unused. `w_qkv`: every entry lies within 4 / sqrt(4096) in magnitude.
All inputs are finite; a program needn't handle non-finite values.
Results may differ from a plain program's by a relative error of at most 0.014.
The roundings to bfloat16 on the way count: a program that leaves them out, or rounds other values in their place, can miss the bound.
Values may be sent and summed in bfloat16 or wider, within the bound.
A program may use at most 64 MiB of HBM per device.

v0:
```python
import math

import jax
import jax.numpy as jnp
from jax import lax
from jax.sharding import PartitionSpec as P


def passed_along(shard, axis, by):
    devices = lax.axis_size(axis)
    pairs = [(i, i + by) for i in range(devices) if 0 <= i + by < devices]
    return lax.ppermute(shard, axis, pairs)


def window_slices(source, starts, length_total):
    return jnp.stack(
        [
            lax.dynamic_slice_in_dim(source, starts[slot], length_total, 0)
            for slot in range(starts.shape[0])
        ],
        axis=0,
    )


def add_windows(buffer, pieces, starts):
    for slot in range(starts.shape[0]):
        placed = lax.dynamic_slice_in_dim(buffer, starts[slot], pieces.shape[1], 0) + pieces[slot]
        buffer = lax.dynamic_update_slice_in_dim(buffer, placed, starts[slot], 0)
    return buffer


def shards(frames, cotangent, w_qkv, w_out, starts, counts):
    frame_count = frames.shape[0]
    slot_count = starts.shape[0]
    window = cotangent.shape[1]
    head_size = w_qkv.shape[2] // 3
    slice_column_width = frames.shape[1]
    scale = 1.0 / math.sqrt(head_size)
    query_key_value_panel, out_panel = (
        lax.all_gather(w_qkv, "video", axis=0, tiled=True),
        lax.all_gather(w_out, "video", axis=0, tiled=True),
    )
    borrowed = passed_along(frames[:window], "video", -1)
    extended = lax.all_gather(jnp.concatenate([frames, borrowed], axis=0), "mp", axis=1, tiled=True)
    window_rows = window_slices(extended, starts, window)
    window_blocks = jnp.einsum(
        "cwd,dhe->cwhe", window_rows, query_key_value_panel, preferred_element_type=jnp.float32
    ).astype(jnp.bfloat16)
    queries = window_blocks[..., :head_size]
    key_vectors = window_blocks[..., head_size : 2 * head_size]
    value_vectors = window_blocks[..., 2 * head_size :]
    scores = (
        jnp.einsum("cqhe,ckhe->chqk", queries, key_vectors, preferred_element_type=jnp.float32)
        * scale
    )
    attention = jax.nn.softmax(scores, axis=-1)
    attention_low = attention.astype(jnp.bfloat16)
    grad_heads = jnp.einsum(
        "cwd,ehd->cwhe", cotangent, out_panel, preferred_element_type=jnp.float32
    ).astype(jnp.bfloat16)
    grad_values = jnp.einsum(
        "chqk,cqhe->ckhe", attention_low, grad_heads, preferred_element_type=jnp.float32
    ).astype(jnp.bfloat16)
    grad_attention = jnp.einsum(
        "cqhe,ckhe->chqk", grad_heads, value_vectors, preferred_element_type=jnp.float32
    )
    centre = jnp.sum(attention * grad_attention, axis=-1, keepdims=True)
    grad_scores = (attention * (grad_attention - centre) * scale).astype(jnp.bfloat16)
    grad_queries = jnp.einsum(
        "chqk,ckhe->cqhe", grad_scores, key_vectors, preferred_element_type=jnp.float32
    ).astype(jnp.bfloat16)
    grad_keys = jnp.einsum(
        "chqk,cqhe->ckhe", grad_scores, queries, preferred_element_type=jnp.float32
    ).astype(jnp.bfloat16)
    live = jnp.arange(slot_count) < counts[0]
    grad_qkv = jnp.concatenate([grad_queries, grad_keys, grad_values], axis=-1)
    grad_qkv = jnp.where(live[:, None, None, None], grad_qkv, jnp.zeros_like(grad_qkv))
    partial_rows = jnp.einsum(
        "cwhe,dhe->cwd", grad_qkv, query_key_value_panel, preferred_element_type=jnp.float32
    )
    accumulated = jnp.zeros((frame_count + window, partial_rows.shape[2]), jnp.float32)
    accumulated = add_windows(accumulated, partial_rows, starts)
    summed = lax.psum_scatter(
        accumulated.astype(jnp.bfloat16), "mp", scatter_dimension=1, tiled=True
    ).astype(jnp.float32)
    offset = lax.axis_index("mp") * slice_column_width
    own_cotangent = lax.dynamic_slice_in_dim(cotangent, offset, slice_column_width, 2).astype(
        jnp.float32
    )
    own_cotangent = jnp.where(live[:, None, None], own_cotangent, jnp.zeros_like(own_cotangent))
    summed = add_windows(summed, own_cotangent, starts)
    carried = passed_along(summed[frame_count:].astype(jnp.bfloat16), "video", 1).astype(
        jnp.float32
    )
    return summed[:frame_count] + jnp.pad(carried, ((0, frame_count - window), (0, 0)))


def solution(mesh):
    placed = (
        P("video", "mp"),
        P("video", None, None),
        P("video", "mp", None),
        P("video", "mp", None),
        P("video"),
        P("video"),
    )
    return jax.shard_map(
        shards, mesh=mesh, in_specs=placed, out_specs=P("video", "mp"), check_vma=False
    )
```

profile of v0, /device:TPU:56, one launch (start us, length us, event | category | flops | bytes accessed | tf_op | source)
XLA Modules:
  0.0 486.2 jit_solution(1263311739536217864)
XLA Ops:
  6.5 0.7 all-gather.8.cloned.1.call-update
  7.3 0.9 slice.57
  8.2 15.4 %collective-permute-start = (bf16[128,512]{1,0:T(8,128)(2,1)S(1)}, bf16[128,512]{1,0:T(8,128)(2,1)S(1)}, u32[]{:S(2)}, u32[]{:S(2)}) collective-permute-start(bf16[128,512]{1,0:T(8,128)(2,1)S(1)} %slice.57), channel_id=1, source_target_pairs={{8,0},{16,8},{24,16},{32,24},{40,32},{48,40},{56,48},{64,56},{72,6... | collective-permute-start | bytes 393224 | tf_op jit(solution)/shard_map/ppermute | solution.py:12
  23.6 2.7 collective-permute-done
  26.3 1.7 pad_maximum_fusion
  28.1 1.5 copy.10
  29.8 1.4 fusion.89
  37.5 109.7 %all-gather.8.cloned.1.call-done = bf16[128,2,4096]{2,1,0:T(2,128)(2,1)} async-done(((bf16[2,2,4096]{2,1,0:T(2,128)(2,1)}), bf16[128,2,4096]{2,1,0:T(2,128)(2,1)}) %all-gather.8.cloned.1.call-update) | async-done | bytes 2097168 | tf_op jit(solution)/shard_map/all_gather | solution.py:41
  147.2 5.3 %fusion.35 = bf16[3,128,2,128]{1,3,0,2:T(8,128)(2,1)S(1)} fusion(bf16[3,128,4096]{2,1,0:T(8,128)(2,1)} %param.7, bf16[128,2,4096,1]{2,1,0,3:T(2,128)(2,1)} %bitcast.68), kind=kOutput, calls=%fused_computation.35 | convolution fusion | flops 805404672 | bytes 5439488 | tf_op jit(solution)/shard_map/cwd,ehd->cwhe/dot_general | solution.py:58
  152.5 39.6 %all-gather.4.cloned.1.call-done = bf16[384,4096]{1,0:T(8,128)(2,1)} async-done(((bf16[384,512]{1,0:T(8,128)(2,1)}), bf16[384,4096]{1,0:T(8,128)(2,1)}) %all-gather.4.cloned.1.call-update) | async-done | bytes 3145744 | tf_op jit(solution)/shard_map/all_gather | solution.py:44
  192.1 2.7 dynamic-slice_bitcast_fusion.2
  194.9 167.2 %all-gather.6.cloned.1.call-done = bf16[4096,2,384]{2,0,1:T(8,128)(2,1)} async-done(((bf16[64,2,384]{2,0,1:T(8,128)(2,1)}), bf16[4096,2,384]{2,0,1:T(8,128)(2,1)}) %all-gather.6.cloned.1.call-update) | async-done | bytes 6291472 | tf_op jit(solution)/shard_map/all_gather | solution.py:40
  362.0 6.2 %fusion.18 = bf16[3,128,2,384]{3,1,2,0:T(8,128)(2,1)} fusion(bf16[4096,2,384]{2,0,1:T(8,128)(2,1)} %all-gather.6.cloned.1.call-done, bf16[1,128,4096]{2,1,0:T(8,128)(2,1)S(1)} %get-tuple-element.6, bf16[1,128,4096]{2,1,0:T(8,128)(2,1)S(1)} %get-tuple-element.7, bf16[1,128,4096]{2,1,0:T(8,128)(2,1)S(1)} %get-tuple-element.5), kind=kOutput, calls=%fused_computation.20 | convolution fusion | flops 2425651200 | bytes 10027008 | tf_op jit(solution)/shard_map/cwd,dhe->cwhe/dot_general | solution.py:46
  368.2 1.4 fusion.90
  369.6 1.1 fusion.53
  370.8 1.2 fusion.32
  372.3 0.4 fusion.33
  372.7 4.8 fusion.6
  377.5 2.6 copy-done
  380.3 3.4 broadcast_in_dim.30
  383.7 6.4 %dynamic_update_slice.18 = f32[384,4096]{1,0:T(8,128)} dynamic-update-slice(f32[384,4096]{1,0:T(8,128)} %broadcast_in_dim.30, f32[128,4096]{1,0:T(8,128)S(1)} %slice_bitcast_fusion.2, s32[]{:T(128)S(6)} %select_n.16, s32[]{:T(128)} %constant.10.clone.1) | dynamic-update-slice | bytes 4194308 | tf_op jit(solution)/shard_map/dynamic_update_slice | solution.py:28
  390.1 2.5 fusion.16
  392.6 6.4 %dynamic_update_slice.19 = f32[384,4096]{1,0:T(8,128)} dynamic-update-slice(f32[384,4096]{1,0:T(8,128)} %dynamic_update_slice.18, f32[128,4096]{1,0:T(8,128)S(1)} %fusion.16, s32[]{:T(128)S(6)} %select_n.17, s32[]{:T(128)} %constant.10.clone.1) | dynamic-update-slice | bytes 4194308 | tf_op jit(solution)/shard_map/dynamic_update_slice | solution.py:28
  399.0 2.5 fusion.15
  401.5 6.4 %dynamic_update_slice.20 = f32[384,4096]{1,0:T(8,128)} dynamic-update-slice(f32[384,4096]{1,0:T(8,128)} %dynamic_update_slice.19, f32[128,4096]{1,0:T(8,128)S(1)} %fusion.15, s32[]{:T(128)S(6)} %select_n.18, s32[]{:T(128)} %constant.10.clone.1) | dynamic-update-slice | bytes 4194308 | tf_op jit(solution)/shard_map/dynamic_update_slice | solution.py:28
  407.9 4.9 %convert_element_type.57 = bf16[384,4096]{1,0:T(8,128)(2,1)} convert(f32[384,4096]{1,0:T(8,128)} %dynamic_update_slice.20) | non-fusion elementwise | flops 1572864 | bytes 9437184 | tf_op jit(solution)/shard_map/convert_element_type | solution.py:84
  412.9 1.1 convert_select_fusion
  414.0 47.3 %reduce-scatter.2.cloned.1.call-done = bf16[384,512]{1,0:T(8,128)(2,1)} async-done(((bf16[384,4096]{1,0:T(8,128)(2,1)}), bf16[384,512]{1,0:T(8,128)(2,1)}) %reduce-scatter.2.cloned.1.call-update) | async-done | bytes 393232 | tf_op jit(solution)/shard_map/reduce_scatter | solution.py:83
  461.3 1.1 convert_element_type.58
  463.7 3.6 collective-permute-start.1
  467.4 11.5 %collective-permute-done.1 = bf16[128,512]{1,0:T(8,128)(2,1)S(1)} collective-permute-done((bf16[128,512]{1,0:T(8,128)(2,1)S(1)}, bf16[128,512]{1,0:T(8,128)(2,1)S(1)}, u32[]{:S(2)}, u32[]{:S(2)}) %collective-permute-start.1) | collective-permute-done | bytes 131104 | tf_op jit(solution)/shard_map/ppermute | solution.py:12
  478.8 0.9 slice_add_fusion
  (20 shorter events, 1.9 us)
Async XLA Ops:
  6.5 140.7 %all-gather.8.cloned.1.call-start = ((), (), s32[]{:S(2)}) async-start(), calls=%async_computation.3 | async-start | bytes 2129920 | tf_op jit(solution)/shard_map/all_gather | solution.py:41
  7.3 184.9 %all-gather.4.cloned.1.call-start = ((), (), s32[]{:S(2)}) async-start(), calls=%async_computation.1 | async-start | bytes 3538944 | tf_op jit(solution)/shard_map/all_gather | solution.py:44
  8.2 18.1 %collective-permute-start = (bf16[128,512]{1,0:T(8,128)(2,1)S(1)}, bf16[128,512]{1,0:T(8,128)(2,1)S(1)}, u32[]{:S(2)}, u32[]{:S(2)}) collective-permute-start(bf16[128,512]{1,0:T(8,128)(2,1)S(1)} %slice.57), channel_id=1, source_target_pairs={{8,0},{16,8},{24,16},{32,24},{40,32},{48,40},{56,48},{64,56},{72,6... | collective-permute-start | bytes 393224 | tf_op jit(solution)/shard_map/ppermute | solution.py:12
  28.1 334.0 %all-gather.6.cloned.1.call-start = ((), (), s32[]{:S(2)}) async-start(), calls=%async_computation.2 | async-start | bytes 6389760 | tf_op jit(solution)/shard_map/all_gather | solution.py:40
  29.7 431.6 %reduce-scatter.2.cloned.1.call-start = ((), (), s32[]{:S(2)}) async-start(), calls=%async_computation.4 | async-start | bytes 3538944 | tf_op jit(solution)/shard_map/reduce_scatter | solution.py:83
  368.2 3.8 copy-start.1
  377.5 2.7 copy-start
  463.7 15.1 %collective-permute-start.1 = (bf16[128,512]{1,0:T(8,128)(2,1)S(1)}, bf16[128,512]{1,0:T(8,128)(2,1)S(1)}, u32[]{:S(2)}, u32[]{:S(2)}) collective-permute-start(bf16[128,512]{1,0:T(8,128)(2,1)S(1)} %slice.127), channel_id=1, source_target_pairs={{0,8},{8,16},{16,24},{24,32},{32,40},{40,48},{48,56},{56,64},{64,7... | collective-permute-start | bytes 393224 | tf_op jit(solution)/shard_map/ppermute | solution.py:12
Sparse Core Ops, SparseCore 0:
  12.0 135.1 all-gather.7
  149.3 42.7 all-gather.3
  196.6 165.3 all-gather.5
  413.0 48.2 reduce-scatter.1
where the time goes:
time: 490 us; the launch traced here: 486 us
  waiting for transfers between devices  379 us (77%)
  local copies, waits for them, and re-layouts  33.2 us (7%)
  matrix products  20.7 us (4%)
  between operations  19.6 us (4%)
  starting transfers between devices  19.1 us (4%)
  other arithmetic  14.8 us (3%)
    all_gather x1, waiting for transfers between devices, shards(): lax.all_gather(w_qkv, 'video', axis=0, tiled=True)  167 us
    all_gather x1, waiting for transfers between devices, shards(): lax.all_gather(w_out, 'video', axis=0, tiled=True)  110 us
    reduce_scatter x1, waiting for transfers between devices, shards(): lax.psum_scatter(accumulated.astype(jnp.bfloat16), 'mp', scatter_dimensio...  47.3 us
    all_gather x1, waiting for transfers between devices, shards(): lax.all_gather(jnp.concatenate([frames, borrowed], axis=0), 'mp', axis=1,...  39.6 us
    dynamic_update_slice x6, local copies, waits for them, and re-layouts, add_windows(): buffer = lax.dynamic_update_slice_in_dim(buffer, placed, starts[slot], 0)  20.4 us
    ppermute x2, starting transfers between devices, passed_along(): return lax.ppermute(shard, axis, pairs)  19 us
    ppermute x2, waiting for transfers between devices, passed_along(): return lax.ppermute(shard, axis, pairs)  14.2 us
  transfers between devices with their start and end apart: 6, of which 6 were waited for; matrix products, arithmetic and copies ran while one was open for 3% of the time, Pallas kernels for 0%

commit v1 on v0

v1 whole, which is shorter than its diff:
```python
import math

import jax
import jax.numpy as jnp
from jax import lax
from jax.experimental import pallas as pl
from jax.experimental.pallas import tpu as pltpu
from jax.sharding import PartitionSpec as P

HIGH, XS, ZS, LOW, CORES = 2, 4, 8, 4, 2
VIDEO = HIGH * XS * ZS
MP = LOW * CORES
MAX_COPIES = 160
MAX_LOCAL = 16
MESH = pl.DeviceIdType.MESH
NT = (((1,), (1,)), ((), ()))
TN = (((0,), (0,)), ((), ()))
F32, BF16 = jnp.float32, jnp.bfloat16


def dot(a, b, dims=(((1,), (0,)), ((), ()))):
    return lax.dot_general(a, b, dims, preferred_element_type=F32)


def kernel(
    starts, counts, frames, cotangent, first_shard, second_shard, out,
    wa, wb, ext, cot, wide, proj_a, proj_b, low, rows, heads, grads, placed,
    direct, own, give, take, part, summed, tail, tail_in, result,
    send_sems, recv_sems, local_sems,
):
    slots = starts.shape[0]
    frame_count, slab = frames.shape
    window = ext.shape[2] - frame_count
    total = ext.shape[2]
    shard_rows = first_shard.shape[0]
    size = proj_a.shape[1]
    qkv_b = proj_b.shape[1]
    piece = wa.shape[4] - size
    out_rows = wide.shape[1]
    scale = 1.0 / math.sqrt(size)

    video, mp = lax.axis_index("video"), lax.axis_index("mp")
    yh, x, z = video // (XS * ZS), (video // ZS) % XS, video % ZS
    yl, c = mp // CORES, mp % CORES
    other = 1 - yh
    xs = [(x + i) % XS for i in range(XS)]
    zs = [(z + i) % ZS for i in range(ZS)]
    yls = [(yl + i) % LOW for i in range(LOW)]
    before, after = (video + VIDEO - 1) % VIDEO, (video + 1) % VIDEO

    def at(video_at, mp_at):
        return {"video": video_at, "mp": mp_at}

    def place(yh_at, x_at, z_at):
        return (yh_at * XS + x_at) * ZS + z_at

    partner = at(place(other, x, z), mp)
    to_x = {1: at(place(yh, xs[1], z), mp), -1: at(place(yh, xs[-1], z), mp)}
    to_z = {1: at(place(yh, x, zs[1]), mp), -1: at(place(yh, x, zs[-1]), mp)}
    sibling = at(video, yl * CORES + 1 - c)

    met = [partner, to_x[1], to_x[-1], to_z[1], to_z[-1], sibling]
    met += [at(video, yls[d] * CORES + c) for d in range(1, LOW)]
    met += [at(side, yls[d] * CORES + c) for d in range(LOW) for side in (before, after)]
    barrier = pltpu.get_barrier_semaphore()
    for device in met:
        pl.semaphore_signal(barrier, inc=1, device_id=device, device_id_type=MESH)

    locals_ = []

    def stage(src, dst):
        copy = pltpu.make_async_copy(src, dst, local_sems.at[len(locals_)])
        copy.start()
        locals_.append(copy)
        return copy

    own_a = stage(first_shard, wa.at[yh, x, z])
    own_b = stage(second_shard, wb.at[yh, x, z])
    own_frames = stage(frames, ext.at[yl, c, pl.ds(0, frame_count)])
    cot_in = [stage(cotangent.at[:, pl.ds(u * slab, slab)], cot.at[u]) for u in range(MP)]

    pl.semaphore_wait(barrier, len(met))

    copies = []

    def push(src, dst, device):
        k = len(copies)
        copy = pltpu.make_async_remote_copy(
            src_ref=src, dst_ref=dst, send_sem=send_sems.at[k], recv_sem=recv_sems.at[k],
            device_id=device, device_id_type=MESH,
        )
        copy.start()
        copies.append(copy)
        return copy

    def same(ref, device):
        return push(ref, ref, device)

    dirs = (1, -1)

    pair_b = push(second_shard, wb.at[yh, x, z], partner)
    pair_a = push(first_shard, wa.at[yh, x, z], partner)
    bz, bx, az, ax, axf = {}, {}, {}, {}, {}
    for s in dirs:
        bz[s, 1] = [push(second_shard, wb.at[yh, x, z], to_z[s])]
    for s in dirs:
        ax[s] = [push(first_shard, wa.at[yh, x, z], to_x[s])]
    for s in dirs:
        bx[s, 0] = [push(second_shard, wb.at[yh, x, z], to_x[s])]

    body = pl.ds(0, frame_count)
    edge = pl.ds(frame_count, window)
    mine = ext.at[yl, c, body]
    far = {d: push(frames, mine, at(video, yls[d] * CORES + c)) for d in (2, 3, 1)}
    lent = {
        d: push(frames.at[pl.ds(0, window)], ext.at[yl, c, edge], at(before, yls[d] * CORES + c))
        for d in (2, 3, 1, 0)
    }

    pair_b.wait_recv()
    for s in dirs:
        bz[s, 1].append(same(wb.at[other, x, z], to_z[s]))
    pair_a.wait_recv()
    for s in dirs:
        ax[s].append(same(wa.at[other, x, z], to_x[s]))
    for s in dirs:
        bx[s, 0].append(same(wb.at[other, x, z], to_x[s]))

    def a_step(step, i):
        for s in dirs:
            z_at = zs[(-s * step) % ZS]
            if step < ZS // 2 - 1:
                ref = wa.at[:, xs[i], z_at]
            else:
                ref = wa.at[0 if s > 0 else 1, xs[i], z_at]
            az[s, step + 1, i] = same(ref, to_z[s])

    own_a.wait()
    a_step(0, 0)

    def b_arrive(step):
        for s in dirs:
            for copy in bz[s, step]:
                copy.wait_recv()
            z_at = zs[(-s * step) % ZS]
            if step < ZS // 2 - 1:
                bz[s, step + 1] = [same(wb.at[:, x, z_at], to_z[s])]
            elif step < ZS // 2:
                bz[s, step + 1] = [same(wb.at[0 if s > 0 else 1, x, z_at], to_z[s])]
        offsets = [-step % ZS, step % ZS] if step < ZS // 2 else [ZS // 2]
        for offset in offsets:
            for s in dirs:
                bx[s, offset] = [same(wb.at[:, x, zs[offset]], to_x[s])]

    bxf = {}

    def b_cross(offset):
        for s in dirs:
            for copy in bx[s, offset]:
                copy.wait_recv()
            ref = wb.at[0 if s > 0 else 1, xs[-s % XS], zs[offset]]
            bxf[s, offset] = same(ref, to_x[s])

    b_arrive(1)
    for s in dirs:
        for copy in ax[s]:
            copy.wait_recv()
        axf[s] = same(wa.at[0 if s > 0 else 1, xs[-s % XS], z], to_x[s])
    a_step(0, 1)
    a_step(0, 3)
    b_arrive(2)
    for s in dirs:
        axf[s].wait_recv()
    a_step(0, 2)
    own_b.wait()
    b_cross(0)
    b_arrive(3)
    b_arrive(4)

    order = (0, 1, 3, 2)

    def a_arrive(step, i):
        for s in dirs:
            az[s, step, i].wait_recv()
        a_step(step, i)

    def share(d):
        if d == 0:
            own_frames.wait()
        else:
            far[d].wait_recv()
        lent[d].wait_recv()
        return same(ext.at[yls[-d % LOW], c], sibling)

    shared = []
    b_cross(7)
    a_arrive(1, 0)
    b_cross(1)
    a_arrive(1, 1)
    a_arrive(1, 3)
    b_cross(6)
    a_arrive(1, 2)
    shared.append(share(0))
    b_cross(2)
    a_arrive(2, 0)
    a_arrive(2, 1)
    b_cross(5)
    shared.append(share(1))
    a_arrive(2, 3)
    b_cross(3)
    a_arrive(2, 2)
    b_cross(4)
    shared.append(share(3))
    for i in order:
        a_arrive(3, i)
    shared.append(share(2))

    for copy in cot_in:
        copy.wait()

    r = lax.broadcasted_iota(jnp.int32, (total, window), 0)
    w = lax.broadcasted_iota(jnp.int32, (total, window), 1)
    put = jnp.concatenate(
        [jnp.where((r - w == starts[j]) & (j < counts[0]), 1.0, 0.0).astype(BF16) for j in range(slots)],
        axis=1,
    )
    direct[...] = dot(put, cot[mp])

    for copy in shared:
        copy.wait_recv()
    for s in dirs:
        for i in order:
            az[s, ZS // 2, i].wait_recv()
        for offset in range(ZS):
            bxf[s, offset].wait_recv()

    proj_a[...] = jnp.zeros_like(proj_a)
    proj_b[...] = jnp.zeros_like(proj_b)

    @pl.loop(0, MP)
    def _(u):
        block = ext[u // CORES, u % CORES]
        weights_b = wb[u // XS, u % XS].reshape(ZS * shard_rows, qkv_b)
        weights_a = wa[u // XS, u % XS]
        proj_b[...] += dot(block, weights_b)
        proj_a[...] += dot(block, weights_a[:, :, :size].reshape(ZS * shard_rows, size))
        wide[pl.ds(u * ZS * 2, ZS * 2)] = (
            weights_a[:, :, size:].astype(F32).reshape(ZS * 2, out_rows, piece)
        )

    low[:, :qkv_b] = proj_b[...].astype(BF16)
    low[:, qkv_b:] = proj_a[...].astype(BF16)
    rows[...] = dot(put, low[...], TN).astype(BF16)

    parts = slab // piece
    count = MP * parts
    acc = jnp.zeros((slots * window, 2 * size), F32)
    for k in range(count):
        block = cot[k // parts, :, (k % parts) * piece:(k % parts + 1) * piece]
        weights = jnp.concatenate(
            [wide[:, h * count + k, :].astype(BF16) for h in range(2)], axis=0
        )
        acc += dot(block, weights, NT)
    heads[...] = acc.astype(BF16)

    for j in range(slots):
        span = slice(j * window, (j + 1) * window)
        for h in range(2):
            base = h * 3 * size
            queries = rows[span, base:base + size]
            keys = rows[span, base + size:base + 2 * size]
            values = rows[span, base + 2 * size:base + 3 * size]
            grad_head = heads[span, h * size:(h + 1) * size]
            scores = dot(queries, keys, NT) * scale
            powers = jnp.exp(scores - jnp.max(scores, axis=-1, keepdims=True))
            attention = powers / jnp.sum(powers, axis=-1, keepdims=True)
            grad_values = dot(attention.astype(BF16), grad_head, TN)
            grad_attention = dot(grad_head, values, NT)
            centre = jnp.sum(attention * grad_attention, axis=-1, keepdims=True)
            grad_scores = (attention * (grad_attention - centre) * scale).astype(BF16)
            grads[span, base:base + size] = dot(grad_scores, keys).astype(BF16)
            grads[span, base + size:base + 2 * size] = dot(grad_scores, queries, TN).astype(BF16)
            grads[span, base + 2 * size:base + 3 * size] = grad_values.astype(BF16)

    placed[...] = dot(put, grads[...]).astype(BF16)

    def group_part(yl_at, c_at):
        u = yl_at * CORES + c_at
        weights_b = wb[u // XS, u % XS].reshape(ZS * shard_rows, qkv_b)
        weights_a = wa[u // XS, u % XS, :, :, :size].reshape(ZS * shard_rows, size)
        return dot(placed[:, :qkv_b], weights_b, NT) + dot(placed[:, qkv_b:], weights_a, NT)

    sums = (2, 3, 1, 0)
    crossing = {}
    for d in sums:
        give[d] = group_part(yls[d], 1 - c).astype(BF16)
        crossing[d] = push(give.at[d], take.at[d], sibling)
    edges, bodies = {}, {}
    for d in sums:
        own[...] = group_part(yls[d], c).astype(BF16).astype(F32)
        crossing[d].wait_recv()
        if d == 0:
            direct[...] += own[...] + take[d].astype(F32)
        else:
            part[d - 1] = (own[...] + take[d].astype(F32)).astype(BF16)
            target = at(video, yls[d] * CORES + c)
            edges[d] = push(part.at[d - 1, edge], summed.at[d - 1, edge], target)
    for d in (2, 3, 1):
        target = at(video, yls[d] * CORES + c)
        bodies[d] = push(part.at[d - 1, body], summed.at[d - 1, body], target)
    for d in (2, 3, 1):
        edges[d].wait_recv()
    over = direct[frame_count:]
    for d in range(1, LOW):
        over += summed[d - 1, frame_count:].astype(F32)
    tail[...] = over.astype(BF16)
    carried = push(tail, tail_in, at(after, mp))
    for d in (2, 3, 1):
        bodies[d].wait_recv()
    keep = direct[:frame_count]
    for d in range(1, LOW):
        keep += summed[d - 1, :frame_count].astype(F32)
    result[...] = keep
    carried.wait_recv()
    result[:window] += jnp.where(video > 0, tail_in[...].astype(F32), 0.0)
    done = pltpu.make_async_copy(result, out, local_sems.at[MAX_LOCAL - 1])
    done.start()
    for copy in copies:
        copy.wait_send()
    done.wait()


def shards(frames, cotangent, w_qkv, w_out, starts, counts):
    frame_count, slab = frames.shape
    slots, window, width = cotangent.shape
    shard_rows, group, qkv = w_qkv.shape
    size = qkv // 3
    total = frame_count + window
    all_qkv = group * qkv
    qkv_b = all_qkv - size
    out_width = w_out.shape[0] * group * width // shard_rows
    flat = w_qkv.reshape(shard_rows, all_qkv)
    second = flat[:, :qkv_b]
    first = jnp.concatenate([flat[:, qkv_b:], w_out.reshape(shard_rows, out_width)], axis=1)
    out_rows = group * width // out_width
    smem = pl.BlockSpec(memory_space=pltpu.SMEM)
    hbm = pl.BlockSpec(memory_space=pl.ANY)
    vmem = pltpu.VMEM
    return pl.pallas_call(
        kernel,
        out_shape=jax.ShapeDtypeStruct((frame_count, slab), F32),
        in_specs=[smem, smem, hbm, hbm, hbm, hbm],
        out_specs=hbm,
        scratch_shapes=[
            vmem((HIGH, XS, ZS, shard_rows, size + out_width), BF16),
            vmem((HIGH, XS, ZS, shard_rows, qkv_b), BF16),
            vmem((LOW, CORES, total, slab), BF16),
            vmem((MP, slots * window, slab), BF16),
            vmem((size, out_rows, out_width), F32),
            vmem((total, size), F32),
            vmem((total, qkv_b), F32),
            vmem((total, all_qkv), BF16),
            vmem((slots * window, all_qkv), BF16),
            vmem((slots * window, group * size), BF16),
            vmem((slots * window, all_qkv), BF16),
            vmem((total, all_qkv), BF16),
            vmem((total, slab), F32),
            vmem((total, slab), F32),
            vmem((LOW, total, slab), BF16),
            vmem((LOW, total, slab), BF16),
            vmem((LOW - 1, total, slab), BF16),
            vmem((LOW - 1, total, slab), BF16),
            vmem((window, slab), BF16),
            vmem((window, slab), BF16),
            vmem((frame_count, slab), F32),
            pltpu.SemaphoreType.DMA((MAX_COPIES,)),
            pltpu.SemaphoreType.DMA((MAX_COPIES,)),
            pltpu.SemaphoreType.DMA((MAX_LOCAL,)),
        ],
        compiler_params=pltpu.CompilerParams(
            collective_id=0, has_side_effects=True, vmem_limit_bytes=56 * 2**20
        ),
    )(starts, counts, frames, cotangent.reshape(slots * window, width), first, second)


def solution(mesh):
    placed = (
        P("video", "mp"),
        P("video", None, None),
        P("video", "mp", None),
        P("video", "mp", None),
        P("video"),
        P("video"),
    )
    return jax.shard_map(
        shards, mesh=mesh, in_specs=placed, out_specs=P("video", "mp"), check_vma=False
    )
```

time: 490 us -> 146 us (0.30)
  the two profiles are of different devices: /device:TPU:56 before, /device:TPU:17 now
where the time goes in v1:
time: 146 us
  Pallas kernels  140 us (96%)
  local copies, waits for them, and re-layouts  4.21 us (3%)
    pallas_call x1, Pallas kernels, shards(): pl.pallas_call(kernel, out_shape=jax.ShapeDtypeStruct((frame_count, slab)...  140 us

profile of v1, /device:TPU:17, one launch (start us, length us, event | category | flops | bytes accessed | tf_op | source)
XLA Modules:
  0.0 145.9 jit_solution(10878614507396464190)
XLA Ops:
  0.7 0.8 reshape.11
  1.4 0.9 copy.7
  2.4 0.6 slice.9.second_shard
  3.0 0.6 pad_maximum_fusion.first_shard
  3.6 140.4 %shard_map.64 = f32[256,512]{1,0:T(8,128)} custom-call(s32[3]{0:T(128)} %starts.1, s32[1]{0:T(128)S(6)} %copy.9.counts, bf16[256,512]{1,0:T(8,128)(2,1)} %frames.1, bf16[384,4096]{1,0:T(8,128)(2,1)} %bitcast.3, bf16[64,384]{1,0:T(8,128)(2,1)} %pad_maximum_fusion.first_shard, bf16[64,640]{1,0:T(8,128)(2,1)} %slice.9.second_shard), custom_call_target="tpu_custom_call" | custom-call | tf_op jit(solution)/shard_map/pallas_call | solution.py:349
  144.1 1.9 %copy.10 = f32[256,512]{1,0:T(8,128)} copy(f32[256,512]{1,0:T(8,128)} %shard_map.64) | data formatting | bytes 1048576
  (1 shorter events, 0.0 us)

commit v2 on v1

--- a/solution.py
+++ b/solution.py
@@ -10,7 +10,8 @@
 HIGH, XS, ZS, LOW, CORES = 2, 4, 8, 4, 2
 VIDEO = HIGH * XS * ZS
 MP = LOW * CORES
-MAX_COPIES = 160
+MAX_COPIES = 128
+MAX_MAYBE = 32
 MAX_LOCAL = 16
 MESH = pl.DeviceIdType.MESH
 NT = (((1,), (1,)), ((), ()))
@@ -25,7 +26,7 @@
 def kernel(
     starts, counts, frames, cotangent, first_shard, second_shard, out,
     wa, wb, ext, cot, wide, proj_a, proj_b, low, rows, heads, grads, placed,
-    direct, own, give, take, part, summed, tail, tail_in, result,
+    direct, own, give, take, part, near, across, home, tail, tail_in, result,
     send_sems, recv_sems, local_sems,
 ):
     slots = starts.shape[0]
@@ -59,9 +60,17 @@
     to_z = {1: at(place(yh, x, zs[1]), mp), -1: at(place(yh, x, zs[-1]), mp)}
     sibling = at(video, yl * CORES + 1 - c)
 
+    last = LOW - 1
+    lower = yl < LOW // 2
+    line = [jnp.where(lower, b, last - b) for b in range(LOW)]
+    is_end = (yl == 0) | (yl == last)
+    is_mid = jnp.logical_not(is_end)
+    outward = at(video, jnp.where(lower, yl + 1, yl - 1) * CORES + c)
+    inward = at(video, jnp.where(lower, yl + last, yl + 1) % LOW * CORES + c)
+
     met = [partner, to_x[1], to_x[-1], to_z[1], to_z[-1], sibling]
     met += [at(video, yls[d] * CORES + c) for d in range(1, LOW)]
-    met += [at(side, yls[d] * CORES + c) for d in range(LOW) for side in (before, after)]
+    met += [at(before, mp), at(after, mp)]
     barrier = pltpu.get_barrier_semaphore()
     for device in met:
         pl.semaphore_signal(barrier, inc=1, device_id=device, device_id_type=MESH)
@@ -111,11 +120,55 @@
     body = pl.ds(0, frame_count)
     edge = pl.ds(frame_count, window)
     mine = ext.at[yl, c, body]
-    far = {d: push(frames, mine, at(video, yls[d] * CORES + c)) for d in (2, 3, 1)}
-    lent = {
-        d: push(frames.at[pl.ds(0, window)], ext.at[yl, c, edge], at(before, yls[d] * CORES + c))
-        for d in (2, 3, 1, 0)
-    }
+    lent = push(frames.at[pl.ds(0, window)], ext.at[yl, c, edge], at(before, mp))
+
+    def later(src, dst, device):
+        k = MAX_COPIES + len(maybe)
+        copy = pltpu.make_async_remote_copy(
+            src_ref=src, dst_ref=dst, send_sem=send_sems.at[k], recv_sem=recv_sems.at[k],
+            device_id=device, device_id_type=MESH,
+        )
+        maybe.append(copy)
+        return copy
+
+    maybe = []
+    end_out = [later(frames, mine, outward)]
+    mid_out_f = [later(frames, mine, outward)]
+    mid_in_f = [later(frames, mine, inward)]
+    own_edge = ext.at[yl, c, edge]
+    end_out.append(later(own_edge, own_edge, outward))
+    mid_out_f.append(later(own_edge, own_edge, outward))
+    mid_in_f.append(later(own_edge, own_edge, inward))
+    pass_out, pass_mid, pass_far = (
+        later(ext.at[line[b], c], ext.at[line[b], c], device)
+        for b, device in ((0, outward), (2, inward), (3, inward))
+    )
+
+    def frame_start(i):
+        @pl.when(is_end)
+        def _():
+            end_out[i].start()
+
+        @pl.when(is_mid)
+        def _():
+            mid_in_f[i].start()
+            mid_out_f[i].start()
+
+    def frame_pass(i):
+        @pl.when(is_mid)
+        def _():
+            if i == 0:
+                for copy in end_out:
+                    copy.wait_recv()
+                pass_out.start()
+                for copy in mid_out_f:
+                    copy.wait_recv()
+                pass_mid.start()
+            else:
+                pass_out.wait_recv()
+                pass_far.start()
+
+    frame_start(0)
 
     pair_b.wait_recv()
     for s in dirs:
@@ -137,6 +190,8 @@
 
     own_a.wait()
     a_step(0, 0)
+    lent.wait_recv()
+    frame_start(1)
 
     def b_arrive(step):
         for s in dirs:
@@ -169,6 +224,7 @@
     a_step(0, 1)
     a_step(0, 3)
     b_arrive(2)
+    frame_pass(0)
     for s in dirs:
         axf[s].wait_recv()
     a_step(0, 2)
@@ -184,36 +240,36 @@
             az[s, step, i].wait_recv()
         a_step(step, i)
 
-    def share(d):
-        if d == 0:
-            own_frames.wait()
-        else:
-            far[d].wait_recv()
-        lent[d].wait_recv()
-        return same(ext.at[yls[-d % LOW], c], sibling)
-
     shared = []
     b_cross(7)
     a_arrive(1, 0)
     b_cross(1)
+    frame_pass(1)
     a_arrive(1, 1)
     a_arrive(1, 3)
     b_cross(6)
     a_arrive(1, 2)
-    shared.append(share(0))
     b_cross(2)
     a_arrive(2, 0)
     a_arrive(2, 1)
     b_cross(5)
-    shared.append(share(1))
     a_arrive(2, 3)
     b_cross(3)
     a_arrive(2, 2)
-    b_cross(4)
-    shared.append(share(3))
     for i in order:
         a_arrive(3, i)
-    shared.append(share(2))
+    b_cross(4)
+    own_frames.wait()
+
+    @pl.when(is_end)
+    def _():
+        for copy in mid_in_f:
+            copy.wait_recv()
+        pass_mid.wait_recv()
+        pass_far.wait_recv()
+
+    for b in range(LOW):
+        shared.append(same(ext.at[line[b], c], sibling))
 
     for copy in cot_in:
         copy.wait()
@@ -226,31 +282,16 @@
     )
     direct[...] = dot(put, cot[mp])
 
-    for copy in shared:
-        copy.wait_recv()
     for s in dirs:
         for i in order:
             az[s, ZS // 2, i].wait_recv()
-        for offset in range(ZS):
-            bxf[s, offset].wait_recv()
-
-    proj_a[...] = jnp.zeros_like(proj_a)
-    proj_b[...] = jnp.zeros_like(proj_b)
 
     @pl.loop(0, MP)
     def _(u):
-        block = ext[u // CORES, u % CORES]
-        weights_b = wb[u // XS, u % XS].reshape(ZS * shard_rows, qkv_b)
-        weights_a = wa[u // XS, u % XS]
-        proj_b[...] += dot(block, weights_b)
-        proj_a[...] += dot(block, weights_a[:, :, :size].reshape(ZS * shard_rows, size))
+        weights = wa[u // XS, u % XS, :, :, size:]
         wide[pl.ds(u * ZS * 2, ZS * 2)] = (
-            weights_a[:, :, size:].astype(F32).reshape(ZS * 2, out_rows, piece)
+            weights.astype(F32).reshape(ZS * 2, out_rows, piece)
         )
-
-    low[:, :qkv_b] = proj_b[...].astype(BF16)
-    low[:, qkv_b:] = proj_a[...].astype(BF16)
-    rows[...] = dot(put, low[...], TN).astype(BF16)
 
     parts = slab // piece
     count = MP * parts
@@ -262,6 +303,27 @@
         )
         acc += dot(block, weights, NT)
     heads[...] = acc.astype(BF16)
+
+    for copy in shared:
+        copy.wait_recv()
+    for s in dirs:
+        for offset in range(ZS):
+            bxf[s, offset].wait_recv()
+
+    proj_a[...] = jnp.zeros_like(proj_a)
+    proj_b[...] = jnp.zeros_like(proj_b)
+
+    @pl.loop(0, MP)
+    def _(u):
+        block = ext[u // CORES, u % CORES]
+        weights_b = wb[u // XS, u % XS].reshape(ZS * shard_rows, qkv_b)
+        weights_a = wa[u // XS, u % XS, :, :, :size].reshape(ZS * shard_rows, size)
+        proj_b[...] += dot(block, weights_b)
+        proj_a[...] += dot(block, weights_a)
+
+    low[:, :qkv_b] = proj_b[...].astype(BF16)
+    low[:, qkv_b:] = proj_a[...].astype(BF16)
+    rows[...] = dot(put, low[...], TN).astype(BF16)
 
     for j in range(slots):
         span = slice(j * window, (j + 1) * window)
@@ -290,43 +352,118 @@
         weights_a = wa[u // XS, u % XS, :, :, :size].reshape(ZS * shard_rows, size)
         return dot(placed[:, :qkv_b], weights_b, NT) + dot(placed[:, qkv_b:], weights_a, NT)
 
-    sums = (2, 3, 1, 0)
+    chunks = (edge, body)
+    from_end = [[later(part.at[b, t], near.at[b - 1, t], outward) for b in (1, 2, 3)] for t in chunks]
+    from_mid = [[later(part.at[b, t], across.at[3 - b, t], outward) for b in (3, 2)] for t in chunks]
+    to_end = [later(part.at[0, t], home.at[t], inward) for t in chunks]
+
     crossing = {}
-    for d in sums:
-        give[d] = group_part(yls[d], 1 - c).astype(BF16)
-        crossing[d] = push(give.at[d], take.at[d], sibling)
-    edges, bodies = {}, {}
-    for d in sums:
-        own[...] = group_part(yls[d], c).astype(BF16).astype(F32)
-        crossing[d].wait_recv()
-        if d == 0:
-            direct[...] += own[...] + take[d].astype(F32)
-        else:
-            part[d - 1] = (own[...] + take[d].astype(F32)).astype(BF16)
-            target = at(video, yls[d] * CORES + c)
-            edges[d] = push(part.at[d - 1, edge], summed.at[d - 1, edge], target)
-    for d in (2, 3, 1):
-        target = at(video, yls[d] * CORES + c)
-        bodies[d] = push(part.at[d - 1, body], summed.at[d - 1, body], target)
-    for d in (2, 3, 1):
-        edges[d].wait_recv()
-    over = direct[frame_count:]
-    for d in range(1, LOW):
-        over += summed[d - 1, frame_count:].astype(F32)
-    tail[...] = over.astype(BF16)
+
+    def cross(b):
+        give[b] = group_part(line[b], 1 - c).astype(BF16)
+        crossing[b] = push(give.at[b], take.at[b], sibling)
+
+    def merge(b):
+        own[...] = group_part(line[b], c).astype(BF16).astype(F32)
+        crossing[b].wait_recv()
+        own[...] += take[b].astype(F32)
+        part[b] = own[...].astype(BF16)
+        if b < 2:
+            @pl.when(is_end if b == 0 else is_mid)
+            def _():
+                direct[...] += own[...]
+
+    def end_send(*pairs):
+        @pl.when(is_end)
+        def _():
+            for t, b in pairs:
+                from_end[t][b - 1].start()
+
+    cross(3)
+    cross(2)
+    merge(3)
+    end_send((1, 3))
+    cross(1)
+    merge(2)
+    end_send((0, 3), (0, 2))
+    cross(0)
+    merge(1)
+    end_send((0, 1), (1, 2), (1, 1))
+
+    def add(ref, t, other_ref):
+        ref[...] = (ref[...].astype(F32) + other_ref[...].astype(F32)).astype(BF16)
+
+    def mid_out(t, b):
+        from_end[t][b - 1].wait_recv()
+        add(part.at[b, chunks[t]], t, near.at[b - 1, chunks[t]])
+        from_mid[t][3 - b].start()
+
+    def mid_in(t):
+        from_mid[t][0].wait_recv()
+        add(part.at[0, chunks[t]], t, across.at[0, chunks[t]])
+        to_end[t].start()
+
+    def finish(t):
+        @pl.when(is_end)
+        def _():
+            to_end[t].wait_recv()
+            direct[chunks[t]] += home[chunks[t]].astype(F32)
+
+        @pl.when(is_mid)
+        def _():
+            from_mid[t][1].wait_recv()
+            from_end[t][0].wait_recv()
+            direct[chunks[t]] += (
+                near[0, chunks[t]].astype(F32) + across[1, chunks[t]].astype(F32)
+            )
+
+    @pl.when(is_mid)
+    def _():
+        mid_out(1, 3)
+        mid_out(0, 3)
+
+    merge(0)
+
+    @pl.when(is_mid)
+    def _():
+        mid_out(0, 2)
+        mid_in(0)
+
+    finish(0)
+    tail[...] = direct[frame_count:].astype(BF16)
     carried = push(tail, tail_in, at(after, mp))
-    for d in (2, 3, 1):
-        bodies[d].wait_recv()
-    keep = direct[:frame_count]
-    for d in range(1, LOW):
-        keep += summed[d - 1, :frame_count].astype(F32)
-    result[...] = keep
+
+    @pl.when(is_mid)
+    def _():
+        mid_in(1)
+        mid_out(1, 2)
+
+    finish(1)
     carried.wait_recv()
+    result[...] = direct[:frame_count]
     result[:window] += jnp.where(video > 0, tail_in[...].astype(F32), 0.0)
     done = pltpu.make_async_copy(result, out, local_sems.at[MAX_LOCAL - 1])
     done.start()
     for copy in copies:
         copy.wait_send()
+    @pl.when(is_end)
+    def _():
+        for t in range(2):
+            for copy in from_end[t]:
+                copy.wait_send()
+            end_out[t].wait_send()
+
+    @pl.when(is_mid)
+    def _():
+        for t in range(2):
+            for copy in from_mid[t]:
+                copy.wait_send()
+            to_end[t].wait_send()
+            mid_out_f[t].wait_send()
+            mid_in_f[t].wait_send()
+        for copy in (pass_out, pass_mid, pass_far):
+            copy.wait_send()
+
     done.wait()
 
 
@@ -368,13 +505,15 @@
             vmem((total, slab), F32),
             vmem((LOW, total, slab), BF16),
             vmem((LOW, total, slab), BF16),
+            vmem((LOW, total, slab), BF16),
             vmem((LOW - 1, total, slab), BF16),
-            vmem((LOW - 1, total, slab), BF16),
+            vmem((2, total, slab), BF16),
+            vmem((total, slab), BF16),
             vmem((window, slab), BF16),
             vmem((window, slab), BF16),
             vmem((frame_count, slab), F32),
-            pltpu.SemaphoreType.DMA((MAX_COPIES,)),
-            pltpu.SemaphoreType.DMA((MAX_COPIES,)),
+            pltpu.SemaphoreType.DMA((MAX_COPIES + MAX_MAYBE,)),
+            pltpu.SemaphoreType.DMA((MAX_COPIES + MAX_MAYBE,)),
             pltpu.SemaphoreType.DMA((MAX_LOCAL,)),
         ],
         compiler_params=pltpu.CompilerParams(

time: 146 us -> 135 us (0.925)
  the two profiles are of different devices: /device:TPU:17 before, /device:TPU:1 now
where the time goes in v2:
time: 135 us
  Pallas kernels  129 us (96%)
  local copies, waits for them, and re-layouts  4.21 us (3%)
    pallas_call x1, Pallas kernels, shards(): pl.pallas_call(kernel, out_shape=jax.ShapeDtypeStruct((frame_count, slab)...  129 us
    unnamed x2, local copies, waits for them, and re-layouts  2.78 us

profile of v2, /device:TPU:1, one launch (start us, length us, event | category | flops | bytes accessed | tf_op | source)
XLA Modules:
  0.0 134.8 jit_solution(14500959210390383204)
XLA Ops:
  0.7 0.8 reshape.11
  1.4 0.9 copy.7
  2.4 0.6 slice.9.second_shard
  3.0 0.6 pad_maximum_fusion.first_shard
  3.6 129.3 %shard_map.64 = f32[256,512]{1,0:T(8,128)} custom-call(s32[3]{0:T(128)} %starts.1, s32[1]{0:T(128)S(6)} %copy.9.counts, bf16[256,512]{1,0:T(8,128)(2,1)} %frames.1, bf16[384,4096]{1,0:T(8,128)(2,1)} %bitcast.3, bf16[64,384]{1,0:T(8,128)(2,1)} %pad_maximum_fusion.first_shard, bf16[64,640]{1,0:T(8,128)(2,1)} %slice.9.second_shard), custom_call_target="tpu_custom_call" | custom-call | tf_op jit(solution)/shard_map/pallas_call | solution.py:486
  133.0 1.9 %copy.10 = f32[256,512]{1,0:T(8,128)} copy(f32[256,512]{1,0:T(8,128)} %shard_map.64) | data formatting | bytes 1048576
  (1 shorter events, 0.0 us)

commit v3 on v2

--- a/solution.py
+++ b/solution.py
@@ -120,8 +120,6 @@
     body = pl.ds(0, frame_count)
     edge = pl.ds(frame_count, window)
     mine = ext.at[yl, c, body]
-    lent = push(frames.at[pl.ds(0, window)], ext.at[yl, c, edge], at(before, mp))
-
     def later(src, dst, device):
         k = MAX_COPIES + len(maybe)
         copy = pltpu.make_async_remote_copy(
@@ -132,6 +130,13 @@
         return copy
 
     maybe = []
+    first, final = video == 0, video == VIDEO - 1
+    lent = later(frames.at[pl.ds(0, window)], ext.at[yl, c, edge], at(before, mp))
+
+    @pl.when(jnp.logical_not(first))
+    def _():
+        lent.start()
+
     end_out = [later(frames, mine, outward)]
     mid_out_f = [later(frames, mine, outward)]
     mid_in_f = [later(frames, mine, inward)]
@@ -170,6 +175,17 @@
 
     frame_start(0)
 
+    def b_early(q, i):
+        for s in dirs:
+            bz[s, 1][i].wait_recv()
+            ref = wb.at[q, x, zs[-s % ZS]]
+            bz.setdefault((s, 2), []).append(same(ref, to_z[s]))
+        for s in dirs:
+            ref = wb.at[q, x, zs[-s % ZS]]
+            for side in dirs:
+                bx.setdefault((side, -s % ZS), []).append(same(ref, to_x[side]))
+
+    b_early(yh, 0)
     pair_b.wait_recv()
     for s in dirs:
         bz[s, 1].append(same(wb.at[other, x, z], to_z[s]))
@@ -178,6 +194,12 @@
         ax[s].append(same(wa.at[other, x, z], to_x[s]))
     for s in dirs:
         bx[s, 0].append(same(wb.at[other, x, z], to_x[s]))
+
+    def widen(i, z_at):
+        for h in range(HIGH):
+            block = wa[h, xs[i], z_at, :, size:].astype(F32)
+            spot = pl.ds(2 * place(h, xs[i], z_at), 2)
+            wide[spot] = block.reshape(2, out_rows, piece)
 
     def a_step(step, i):
         for s in dirs:
@@ -190,7 +212,15 @@
 
     own_a.wait()
     a_step(0, 0)
-    lent.wait_recv()
+
+    @pl.when(jnp.logical_not(final))
+    def _():
+        lent.wait_recv()
+
+    @pl.when(final)
+    def _():
+        ext[yl, c, frame_count:] = jnp.zeros((window, slab), BF16)
+
     frame_start(1)
 
     def b_arrive(step):
@@ -216,18 +246,21 @@
             ref = wb.at[0 if s > 0 else 1, xs[-s % XS], zs[offset]]
             bxf[s, offset] = same(ref, to_x[s])
 
-    b_arrive(1)
+    b_early(other, 1)
     for s in dirs:
         for copy in ax[s]:
             copy.wait_recv()
         axf[s] = same(wa.at[0 if s > 0 else 1, xs[-s % XS], z], to_x[s])
     a_step(0, 1)
     a_step(0, 3)
+    for i in (0, 1, 3):
+        widen(i, z)
     b_arrive(2)
     frame_pass(0)
     for s in dirs:
         axf[s].wait_recv()
     a_step(0, 2)
+    widen(2, z)
     own_b.wait()
     b_cross(0)
     b_arrive(3)
@@ -239,6 +272,8 @@
         for s in dirs:
             az[s, step, i].wait_recv()
         a_step(step, i)
+        for s in dirs:
+            widen(i, zs[-s * step % ZS])
 
     shared = []
     b_cross(7)
@@ -256,9 +291,6 @@
     a_arrive(2, 3)
     b_cross(3)
     a_arrive(2, 2)
-    for i in order:
-        a_arrive(3, i)
-    b_cross(4)
     own_frames.wait()
 
     @pl.when(is_end)
@@ -270,6 +302,10 @@
 
     for b in range(LOW):
         shared.append(same(ext.at[line[b], c], sibling))
+
+    for i in order:
+        a_arrive(3, i)
+    b_cross(4)
 
     for copy in cot_in:
         copy.wait()
@@ -282,16 +318,32 @@
     )
     direct[...] = dot(put, cot[mp])
 
+    for copy in shared:
+        copy.wait_recv()
+
+    proj_a[...] = jnp.zeros_like(proj_a)
+    proj_b[...] = jnp.zeros_like(proj_b)
+
+    def project_b(i):
+        @pl.loop(0, HIGH)
+        def _(h):
+            u = h * XS + xs[i]
+            weights = wb[h, xs[i]].reshape(ZS * shard_rows, qkv_b)
+            proj_b[...] += dot(ext[u // CORES, u % CORES], weights)
+
+    for i in (0, 1, 3):
+        project_b(i)
+
     for s in dirs:
         for i in order:
             az[s, ZS // 2, i].wait_recv()
+    for i in order:
+        widen(i, zs[ZS // 2])
 
     @pl.loop(0, MP)
     def _(u):
-        weights = wa[u // XS, u % XS, :, :, size:]
-        wide[pl.ds(u * ZS * 2, ZS * 2)] = (
-            weights.astype(F32).reshape(ZS * 2, out_rows, piece)
-        )
+        weights = wa[u // XS, u % XS, :, :, :size].reshape(ZS * shard_rows, size)
+        proj_a[...] += dot(ext[u // CORES, u % CORES], weights)
 
     parts = slab // piece
     count = MP * parts
@@ -304,22 +356,10 @@
         acc += dot(block, weights, NT)
     heads[...] = acc.astype(BF16)
 
-    for copy in shared:
-        copy.wait_recv()
     for s in dirs:
         for offset in range(ZS):
             bxf[s, offset].wait_recv()
-
-    proj_a[...] = jnp.zeros_like(proj_a)
-    proj_b[...] = jnp.zeros_like(proj_b)
-
-    @pl.loop(0, MP)
-    def _(u):
-        block = ext[u // CORES, u % CORES]
-        weights_b = wb[u // XS, u % XS].reshape(ZS * shard_rows, qkv_b)
-        weights_a = wa[u // XS, u % XS, :, :, :size].reshape(ZS * shard_rows, size)
-        proj_b[...] += dot(block, weights_b)
-        proj_a[...] += dot(block, weights_a)
+    project_b(2)
 
     low[:, :qkv_b] = proj_b[...].astype(BF16)
     low[:, qkv_b:] = proj_a[...].astype(BF16)
@@ -382,13 +422,13 @@
     cross(3)
     cross(2)
     merge(3)
-    end_send((1, 3))
+    end_send((0, 3))
     cross(1)
     merge(2)
-    end_send((0, 3), (0, 2))
+    end_send((0, 2))
     cross(0)
     merge(1)
-    end_send((0, 1), (1, 2), (1, 1))
+    end_send((0, 1), (1, 3), (1, 2), (1, 1))
 
     def add(ref, t, other_ref):
         ref[...] = (ref[...].astype(F32) + other_ref[...].astype(F32)).astype(BF16)
@@ -417,35 +457,49 @@
                 near[0, chunks[t]].astype(F32) + across[1, chunks[t]].astype(F32)
             )
 
+    merge(0)
+
     @pl.when(is_mid)
     def _():
-        mid_out(1, 3)
         mid_out(0, 3)
-
-    merge(0)
-
-    @pl.when(is_mid)
-    def _():
         mid_out(0, 2)
         mid_in(0)
 
     finish(0)
     tail[...] = direct[frame_count:].astype(BF16)
-    carried = push(tail, tail_in, at(after, mp))
+    carried = later(tail, tail_in, at(after, mp))
+
+    @pl.when(jnp.logical_not(final))
+    def _():
+        carried.start()
 
     @pl.when(is_mid)
     def _():
+        mid_out(1, 3)
         mid_in(1)
         mid_out(1, 2)
 
     finish(1)
-    carried.wait_recv()
     result[...] = direct[:frame_count]
-    result[:window] += jnp.where(video > 0, tail_in[...].astype(F32), 0.0)
+
+    @pl.when(jnp.logical_not(first))
+    def _():
+        carried.wait_recv()
+        result[:window] += tail_in[...].astype(F32)
+
     done = pltpu.make_async_copy(result, out, local_sems.at[MAX_LOCAL - 1])
     done.start()
     for copy in copies:
         copy.wait_send()
+
+    @pl.when(jnp.logical_not(first))
+    def _():
+        lent.wait_send()
+
+    @pl.when(jnp.logical_not(final))
+    def _():
+        carried.wait_send()
+
     @pl.when(is_end)
     def _():
         for t in range(2):

time: 135 us -> 125 us (0.926)
  the two profiles are of different devices: /device:TPU:1 before, /device:TPU:56 now
where the time goes in v3:
time: 125 us
  Pallas kernels  119 us (95%)
  local copies, waits for them, and re-layouts  4.21 us (3%)
    pallas_call x1, Pallas kernels, shards(): pl.pallas_call(kernel, out_shape=jax.ShapeDtypeStruct((frame_count, slab)...  119 us
    unnamed x2, local copies, waits for them, and re-layouts  2.78 us

profile of v3, /device:TPU:56, one launch (start us, length us, event | category | flops | bytes accessed | tf_op | source)
XLA Modules:
  0.0 124.7 jit_solution(673963395942772103)
XLA Ops:
  0.7 0.8 reshape.11
  1.4 0.9 copy.7
  2.4 0.6 slice.9.second_shard
  3.0 0.6 pad_maximum_fusion.first_shard
  3.6 119.2 %shard_map.64 = f32[256,512]{1,0:T(8,128)} custom-call(s32[3]{0:T(128)} %starts.1, s32[1]{0:T(128)S(6)} %copy.9.counts, bf16[256,512]{1,0:T(8,128)(2,1)} %frames.1, bf16[384,4096]{1,0:T(8,128)(2,1)} %bitcast.3, bf16[64,384]{1,0:T(8,128)(2,1)} %pad_maximum_fusion.first_shard, bf16[64,640]{1,0:T(8,128)(2,1)} %slice.9.second_shard), custom_call_target="tpu_custom_call" | custom-call | tf_op jit(solution)/shard_map/pallas_call | solution.py:540
  122.9 1.9 %copy.10 = f32[256,512]{1,0:T(8,128)} copy(f32[256,512]{1,0:T(8,128)} %shard_map.64) | data formatting | bytes 1048576
  (1 shorter events, 0.0 us)

commit v4 on v3

--- a/solution.py
+++ b/solution.py
@@ -25,7 +25,7 @@
 
 def kernel(
     starts, counts, frames, cotangent, first_shard, second_shard, out,
-    wa, wb, ext, cot, wide, proj_a, proj_b, low, rows, heads, grads, placed,
+    wa, wb, ext, cot, wide, order_rows, proj_a, proj_b, low, rows, heads, grads, placed,
     direct, own, give, take, part, near, across, home, tail, tail_in, result,
     send_sems, recv_sems, local_sems,
 ):
@@ -37,7 +37,7 @@
     size = proj_a.shape[1]
     qkv_b = proj_b.shape[1]
     piece = wa.shape[4] - size
-    out_rows = wide.shape[1]
+    out_rows = 2 * wide.shape[0]
     scale = 1.0 / math.sqrt(size)
 
     video, mp = lax.axis_index("video"), lax.axis_index("mp")
@@ -173,8 +173,6 @@
                 pass_out.wait_recv()
                 pass_far.start()
 
-    frame_start(0)
-
     def b_early(q, i):
         for s in dirs:
             bz[s, 1][i].wait_recv()
@@ -186,6 +184,7 @@
                 bx.setdefault((side, -s % ZS), []).append(same(ref, to_x[side]))
 
     b_early(yh, 0)
+    frame_start(0)
     pair_b.wait_recv()
     for s in dirs:
         bz[s, 1].append(same(wb.at[other, x, z], to_z[s]))
@@ -195,11 +194,23 @@
     for s in dirs:
         bx[s, 0].append(same(wb.at[other, x, z], to_x[s]))
 
-    def widen(i, z_at):
-        for h in range(HIGH):
-            block = wa[h, xs[i], z_at, :, size:].astype(F32)
-            spot = pl.ds(2 * place(h, xs[i], z_at), 2)
-            wide[spot] = block.reshape(2, out_rows, piece)
+    group = HIGH * XS
+    per_shard = shard_rows // out_rows
+    half = out_rows // 2
+    mixed = group * shard_rows
+    to = lax.broadcasted_iota(jnp.int32, (mixed, mixed), 0)
+    source = lax.broadcasted_iota(jnp.int32, (mixed, mixed), 1)
+    each = 2 * group * per_shard
+    inner = to % (group * per_shard)
+    wanted = (
+        inner // per_shard * shard_rows + inner % per_shard * out_rows
+        + to % each // (group * per_shard) * half + to // each
+    )
+    order_rows[...] = jnp.where(source == wanted, 1.0, 0.0).astype(BF16)
+
+    def sort(z_at):
+        block = wa[:, :, z_at, :, size:].reshape(mixed, piece)
+        wide[:, z_at] = dot(order_rows[...], block).astype(BF16).reshape(half, each, piece)
 
     def a_step(step, i):
         for s in dirs:
@@ -246,6 +257,14 @@
             ref = wb.at[0 if s > 0 else 1, xs[-s % XS], zs[offset]]
             bxf[s, offset] = same(ref, to_x[s])
 
+    order = (0, 1, 3, 2)
+
+    def a_arrive(step, i):
+        for s in dirs:
+            az[s, step, i].wait_recv()
+        a_step(step, i)
+
+    shared = []
     b_early(other, 1)
     for s in dirs:
         for copy in ax[s]:
@@ -253,44 +272,30 @@
         axf[s] = same(wa.at[0 if s > 0 else 1, xs[-s % XS], z], to_x[s])
     a_step(0, 1)
     a_step(0, 3)
-    for i in (0, 1, 3):
-        widen(i, z)
+    frame_pass(0)
     b_arrive(2)
-    frame_pass(0)
+    a_arrive(1, 0)
     for s in dirs:
         axf[s].wait_recv()
     a_step(0, 2)
-    widen(2, z)
+    b_cross(0)
+    sort(z)
     own_b.wait()
-    b_cross(0)
     b_arrive(3)
+    a_arrive(1, 1)
+    b_cross(7)
+    a_arrive(1, 3)
     b_arrive(4)
-
-    order = (0, 1, 3, 2)
-
-    def a_arrive(step, i):
-        for s in dirs:
-            az[s, step, i].wait_recv()
-        a_step(step, i)
-        for s in dirs:
-            widen(i, zs[-s * step % ZS])
-
-    shared = []
-    b_cross(7)
-    a_arrive(1, 0)
+    frame_pass(1)
     b_cross(1)
-    frame_pass(1)
-    a_arrive(1, 1)
-    a_arrive(1, 3)
+    a_arrive(1, 2)
+    a_arrive(2, 0)
     b_cross(6)
-    a_arrive(1, 2)
+    sort(zs[1])
+    sort(zs[-1])
+    a_arrive(2, 1)
     b_cross(2)
-    a_arrive(2, 0)
-    a_arrive(2, 1)
-    b_cross(5)
     a_arrive(2, 3)
-    b_cross(3)
-    a_arrive(2, 2)
     own_frames.wait()
 
     @pl.when(is_end)
@@ -298,14 +303,6 @@
         for copy in mid_in_f:
             copy.wait_recv()
         pass_mid.wait_recv()
-        pass_far.wait_recv()
-
-    for b in range(LOW):
-        shared.append(same(ext.at[line[b], c], sibling))
-
-    for i in order:
-        a_arrive(3, i)
-    b_cross(4)
 
     for copy in cot_in:
         copy.wait()
@@ -318,27 +315,48 @@
     )
     direct[...] = dot(put, cot[mp])
 
+
+    def project_b(i, h):
+        u = h * XS + xs[i]
+        weights = wb[h, xs[i]].reshape(ZS * shard_rows, qkv_b)
+        proj_b[...] += dot(ext[u // CORES, u % CORES], weights)
+
+    for b in range(LOW - 1):
+        shared.append(same(ext.at[line[b], c], sibling))
+    b_cross(5)
+    a_arrive(2, 2)
+    sort(zs[2])
+    sort(zs[-2])
+    b_cross(3)
+    a_arrive(3, 0)
+    b_cross(4)
+
+    @pl.when(is_end)
+    def _():
+        pass_far.wait_recv()
+
+    shared.append(same(ext.at[line[LOW - 1], c], sibling))
+    proj_a[...] = jnp.zeros_like(proj_a)
+    proj_b[...] = jnp.zeros_like(proj_b)
+    a_arrive(3, 1)
     for copy in shared:
         copy.wait_recv()
-
-    proj_a[...] = jnp.zeros_like(proj_a)
-    proj_b[...] = jnp.zeros_like(proj_b)
-
-    def project_b(i):
-        @pl.loop(0, HIGH)
-        def _(h):
-            u = h * XS + xs[i]
-            weights = wb[h, xs[i]].reshape(ZS * shard_rows, qkv_b)
-            proj_b[...] += dot(ext[u // CORES, u % CORES], weights)
-
-    for i in (0, 1, 3):
-        project_b(i)
+    project_b(0, 0)
+    project_b(0, 1)
+    a_arrive(3, 3)
+    project_b(1, 0)
+    a_arrive(3, 2)
+    sort(zs[3])
+    sort(zs[-3])
+    project_b(1, 1)
+    project_b(3, 0)
+    project_b(3, 1)
+
 
     for s in dirs:
         for i in order:
             az[s, ZS // 2, i].wait_recv()
-    for i in order:
-        widen(i, zs[ZS // 2])
+    sort(zs[ZS // 2])
 
     @pl.loop(0, MP)
     def _(u):
@@ -346,20 +364,25 @@
         proj_a[...] += dot(ext[u // CORES, u % CORES], weights)
 
     parts = slab // piece
-    count = MP * parts
-    acc = jnp.zeros((slots * window, 2 * size), F32)
-    for k in range(count):
+    acc = jnp.zeros((slots * window, ZS * each), F32)
+    for k in range(half):
         block = cot[k // parts, :, (k % parts) * piece:(k % parts + 1) * piece]
-        weights = jnp.concatenate(
-            [wide[:, h * count + k, :].astype(BF16) for h in range(2)], axis=0
-        )
-        acc += dot(block, weights, NT)
-    heads[...] = acc.astype(BF16)
+        acc += dot(block, wide[k].reshape(ZS * each, piece), NT)
+    n = lax.broadcasted_iota(jnp.int32, (ZS * each, ZS * each), 0)
+    n_to = lax.broadcasted_iota(jnp.int32, (ZS * each, ZS * each), 1)
+    inner = n % (group * per_shard)
+    wanted = (
+        n % each // (group * per_shard) * size
+        + (inner // per_shard * ZS + n // each) * per_shard + inner % per_shard
+    )
+    columns = jnp.where(n_to == wanted, 1.0, 0.0).astype(BF16)
+    heads[...] = dot(acc.astype(BF16), columns).astype(BF16)
 
     for s in dirs:
         for offset in range(ZS):
             bxf[s, offset].wait_recv()
-    project_b(2)
+    for h in range(HIGH):
+        project_b(2, h)
 
     low[:, :qkv_b] = proj_b[...].astype(BF16)
     low[:, qkv_b:] = proj_a[...].astype(BF16)
@@ -547,7 +570,8 @@
             vmem((HIGH, XS, ZS, shard_rows, qkv_b), BF16),
             vmem((LOW, CORES, total, slab), BF16),
             vmem((MP, slots * window, slab), BF16),
-            vmem((size, out_rows, out_width), F32),
+            vmem((out_rows // 2, ZS, 2 * HIGH * XS * shard_rows // out_rows, out_width), BF16),
+            vmem((HIGH * XS * shard_rows, HIGH * XS * shard_rows), BF16),
             vmem((total, size), F32),
             vmem((total, qkv_b), F32),
             vmem((total, all_qkv), BF16),

time: 125 us -> 122 us (0.976)
  Pallas kernels: 119 us -> 116 us
    pallas_call x1, Pallas kernels: 119 us -> 116 us  [shards(): pl.pallas_call(kernel, out_shape=jax.ShapeDtypeStruct((frame_count, slab)...]
where the time goes in v4:
time: 122 us
  Pallas kernels  116 us (95%)
  local copies, waits for them, and re-layouts  4.21 us (3%)
    pallas_call x1, Pallas kernels, shards(): pl.pallas_call(kernel, out_shape=jax.ShapeDtypeStruct((frame_count, slab)...  116 us
    unnamed x2, local copies, waits for them, and re-layouts  2.78 us

profile of v4, /device:TPU:56, one launch (start us, length us, event | category | flops | bytes accessed | tf_op | source)
XLA Modules:
  0.0 121.5 jit_solution(6004042593351469969)
XLA Ops:
  0.7 0.8 reshape.11
  1.4 0.9 copy.7
  2.4 0.6 slice.9.second_shard
  3.0 0.6 pad_maximum_fusion.first_shard
  3.6 116.0 %shard_map.64 = f32[256,512]{1,0:T(8,128)} custom-call(s32[3]{0:T(128)} %starts.1, s32[1]{0:T(128)S(6)} %copy.9.counts, bf16[256,512]{1,0:T(8,128)(2,1)} %frames.1, bf16[384,4096]{1,0:T(8,128)(2,1)} %bitcast.3, bf16[64,384]{1,0:T(8,128)(2,1)} %pad_maximum_fusion.first_shard, bf16[64,640]{1,0:T(8,128)(2,1)} %slice.9.second_shard), custom_call_target="tpu_custom_call" | custom-call | tf_op jit(solution)/shard_map/pallas_call | solution.py:563
  119.6 1.9 %copy.10 = f32[256,512]{1,0:T(8,128)} copy(f32[256,512]{1,0:T(8,128)} %shard_map.64) | data formatting | bytes 1048576
  (1 shorter events, 0.0 us)

commit v5 on v4

--- a/solution.py
+++ b/solution.py
@@ -24,8 +24,8 @@
 
 
 def kernel(
-    starts, counts, frames, cotangent, first_shard, second_shard, out,
-    wa, wb, ext, cot, wide, order_rows, proj_a, proj_b, low, rows, heads, grads, placed,
+    starts, counts, frames, cotangent, w_qkv, w_out, out,
+    first_shard, second_shard, lines, wa, wb, ext, cot, wide, order_rows, proj_a, proj_b, low, rows, heads, grads, placed,
     direct, own, give, take, part, near, across, home, tail, tail_in, result,
     send_sems, recv_sems, local_sems,
 ):
@@ -33,7 +33,7 @@
     frame_count, slab = frames.shape
     window = ext.shape[2] - frame_count
     total = ext.shape[2]
-    shard_rows = first_shard.shape[0]
+    shard_rows = w_qkv.shape[0]
     size = proj_a.shape[1]
     qkv_b = proj_b.shape[1]
     piece = wa.shape[4] - size
@@ -83,10 +83,23 @@
         locals_.append(copy)
         return copy
 
+    own_frames = stage(frames, ext.at[yl, c, pl.ds(0, frame_count)])
+    cot_in = [stage(cotangent.at[:, pl.ds(u * slab, slab)], cot.at[u]) for u in range(MP)]
+
+    qkv = w_qkv[...].astype(F32)
+    panels = w_out[...].astype(F32)
+    head_qkv = 3 * size
+    second_shard[:, :head_qkv] = qkv[:, 0].astype(BF16)
+    second_shard[:, head_qkv:] = qkv[:, 1, :qkv_b - head_qkv].astype(BF16)
+    first_shard[:, :size] = qkv[:, 1, qkv_b - head_qkv:].astype(BF16)
+    for e in range(panels.shape[0]):
+        for h in range(2):
+            for k in range(out_rows // 2):
+                row = (e * 2 + h) * (out_rows // 2) + k
+                lines[row:row + 1] = panels[e, h:h + 1, k * piece:(k + 1) * piece]
+    first_shard[:, size:] = lines[...].astype(BF16)
     own_a = stage(first_shard, wa.at[yh, x, z])
     own_b = stage(second_shard, wb.at[yh, x, z])
-    own_frames = stage(frames, ext.at[yl, c, pl.ds(0, frame_count)])
-    cot_in = [stage(cotangent.at[:, pl.ds(u * slab, slab)], cot.at[u]) for u in range(MP)]
 
     pl.semaphore_wait(barrier, len(met))
 
@@ -553,9 +566,6 @@
     all_qkv = group * qkv
     qkv_b = all_qkv - size
     out_width = w_out.shape[0] * group * width // shard_rows
-    flat = w_qkv.reshape(shard_rows, all_qkv)
-    second = flat[:, :qkv_b]
-    first = jnp.concatenate([flat[:, qkv_b:], w_out.reshape(shard_rows, out_width)], axis=1)
     out_rows = group * width // out_width
     smem = pl.BlockSpec(memory_space=pltpu.SMEM)
     hbm = pl.BlockSpec(memory_space=pl.ANY)
@@ -563,9 +573,12 @@
     return pl.pallas_call(
         kernel,
         out_shape=jax.ShapeDtypeStruct((frame_count, slab), F32),
-        in_specs=[smem, smem, hbm, hbm, hbm, hbm],
+        in_specs=[smem, smem, hbm, hbm, pl.BlockSpec(memory_space=vmem), pl.BlockSpec(memory_space=vmem)],
         out_specs=hbm,
         scratch_shapes=[
+            vmem((shard_rows, size + out_width), BF16),
+            vmem((shard_rows, qkv_b), BF16),
+            vmem((shard_rows, out_width), F32),
             vmem((HIGH, XS, ZS, shard_rows, size + out_width), BF16),
             vmem((HIGH, XS, ZS, shard_rows, qkv_b), BF16),
             vmem((LOW, CORES, total, slab), BF16),
@@ -597,7 +610,7 @@
         compiler_params=pltpu.CompilerParams(
             collective_id=0, has_side_effects=True, vmem_limit_bytes=56 * 2**20
         ),
-    )(starts, counts, frames, cotangent.reshape(slots * window, width), first, second)
+    )(starts, counts, frames, cotangent.reshape(slots * window, width), w_qkv, w_out)
 
 
 def solution(mesh):

time: 122 us -> 119 us (0.975)
  local copies, waits for them, and re-layouts: 4.21 us -> 1.87 us
    unnamed x2 -> x1, local copies, waits for them, and re-layouts: 2.78 us -> 1.87 us
where the time goes in v5:
time: 119 us
  Pallas kernels  116 us (97%)
  local copies, waits for them, and re-layouts  1.87 us (2%)
    pallas_call x1, Pallas kernels, shards(): pl.pallas_call(kernel, out_shape=jax.ShapeDtypeStruct((frame_count, slab)...  116 us

profile of v5, /device:TPU:56, one launch (start us, length us, event | category | flops | bytes accessed | tf_op | source)
XLA Modules:
  0.0 118.6 jit_solution(7567309860513996775)
XLA Ops:
  0.7 116.0 %shard_map.64 = f32[256,512]{1,0:T(8,128)} custom-call(s32[3]{0:T(128)} %starts.1, s32[1]{0:T(128)S(6)} %copy.8.counts, bf16[256,512]{1,0:T(8,128)(2,1)} %frames.1, bf16[384,4096]{1,0:T(8,128)(2,1)} %bitcast.1, bf16[64,2,384]{2,1,0:T(2,128)(2,1)} %w_qkv.1, bf16[2,2,4096]{2,1,0:T(2,128)(2,1)} %w_out.1), custom_call_target="tpu_custom_call" | custom-call | tf_op jit(solution)/shard_map/pallas_call | solution.py:573
  116.7 1.9 %copy.9 = f32[256,512]{1,0:T(8,128)} copy(f32[256,512]{1,0:T(8,128)} %shard_map.64) | data formatting | bytes 1048576

commit v6 on v5

--- a/solution.py
+++ b/solution.py
@@ -211,15 +211,17 @@
     per_shard = shard_rows // out_rows
     half = out_rows // 2
     mixed = group * shard_rows
-    to = lax.broadcasted_iota(jnp.int32, (mixed, mixed), 0)
-    source = lax.broadcasted_iota(jnp.int32, (mixed, mixed), 1)
     each = 2 * group * per_shard
-    inner = to % (group * per_shard)
-    wanted = (
-        inner // per_shard * shard_rows + inner % per_shard * out_rows
-        + to % each // (group * per_shard) * half + to // each
-    )
-    order_rows[...] = jnp.where(source == wanted, 1.0, 0.0).astype(BF16)
+
+    def make_order():
+        to = lax.broadcasted_iota(jnp.int32, (mixed, 1), 0)
+        inner = to % (group * per_shard)
+        wanted = (
+            inner // per_shard * shard_rows + inner % per_shard * out_rows
+            + to % each // (group * per_shard) * half + to // each
+        )
+        source = lax.broadcasted_iota(jnp.int32, (mixed, mixed), 1)
+        order_rows[...] = jnp.where(source == wanted, 1.0, 0.0).astype(BF16)
 
     def sort(z_at):
         block = wa[:, :, z_at, :, size:].reshape(mixed, piece)
@@ -292,6 +294,7 @@
         axf[s].wait_recv()
     a_step(0, 2)
     b_cross(0)
+    make_order()
     sort(z)
     own_b.wait()
     b_arrive(3)
@@ -381,7 +384,7 @@
     for k in range(half):
         block = cot[k // parts, :, (k % parts) * piece:(k % parts + 1) * piece]
         acc += dot(block, wide[k].reshape(ZS * each, piece), NT)
-    n = lax.broadcasted_iota(jnp.int32, (ZS * each, ZS * each), 0)
+    n = lax.broadcasted_iota(jnp.int32, (ZS * each, 1), 0)
     n_to = lax.broadcasted_iota(jnp.int32, (ZS * each, ZS * each), 1)
     inner = n % (group * per_shard)
     wanted = (
@@ -426,7 +429,7 @@
         u = yl_at * CORES + c_at
         weights_b = wb[u // XS, u % XS].reshape(ZS * shard_rows, qkv_b)
         weights_a = wa[u // XS, u % XS, :, :, :size].reshape(ZS * shard_rows, size)
-        return dot(placed[:, :qkv_b], weights_b, NT) + dot(placed[:, qkv_b:], weights_a, NT)
+        return dot(placed[...], jnp.concatenate([weights_b, weights_a], axis=1), NT)
 
     chunks = (edge, body)
     from_end = [[later(part.at[b, t], near.at[b - 1, t], outward) for b in (1, 2, 3)] for t in chunks]
@@ -515,6 +518,23 @@
         mid_in(1)
         mid_out(1, 2)
 
+    for copy in copies:
+        copy.wait_send()
+
+    @pl.when(jnp.logical_not(first))
+    def _():
+        lent.wait_send()
+
+    @pl.when(is_end)
+    def _():
+        for copy in end_out:
+            copy.wait_send()
+
+    @pl.when(is_mid)
+    def _():
+        for copy in (*mid_out_f, *mid_in_f, pass_out, pass_mid, pass_far):
+            copy.wait_send()
+
     finish(1)
     result[...] = direct[:frame_count]
 
@@ -525,13 +545,6 @@
 
     done = pltpu.make_async_copy(result, out, local_sems.at[MAX_LOCAL - 1])
     done.start()
-    for copy in copies:
-        copy.wait_send()
-
-    @pl.when(jnp.logical_not(first))
-    def _():
-        lent.wait_send()
-
     @pl.when(jnp.logical_not(final))
     def _():
         carried.wait_send()
@@ -541,7 +554,6 @@
         for t in range(2):
             for copy in from_end[t]:
                 copy.wait_send()
-            end_out[t].wait_send()
 
     @pl.when(is_mid)
     def _():
@@ -549,10 +561,6 @@
             for copy in from_mid[t]:
                 copy.wait_send()
             to_end[t].wait_send()
-            mid_out_f[t].wait_send()
-            mid_in_f[t].wait_send()
-        for copy in (pass_out, pass_mid, pass_far):
-            copy.wait_send()
 
     done.wait()
 

time: 119 us -> 118 us (level)
  no operation moved by 1% of the time
where the time goes in v6:
time: 118 us
  Pallas kernels  115 us (97%)
  local copies, waits for them, and re-layouts  1.87 us (2%)
    pallas_call x1, Pallas kernels, shards(): pl.pallas_call(kernel, out_shape=jax.ShapeDtypeStruct((frame_count, slab)...  115 us

profile of v6, /device:TPU:56, one launch (start us, length us, event | category | flops | bytes accessed | tf_op | source)
XLA Modules:
  0.0 117.8 jit_solution(7744892037508593038)
XLA Ops:
  0.7 115.2 %shard_map.64 = f32[256,512]{1,0:T(8,128)} custom-call(s32[3]{0:T(128)} %starts.1, s32[1]{0:T(128)S(6)} %copy.8.counts, bf16[256,512]{1,0:T(8,128)(2,1)} %frames.1, bf16[384,4096]{1,0:T(8,128)(2,1)} %bitcast.1, bf16[64,2,384]{2,1,0:T(2,128)(2,1)} %w_qkv.1, bf16[2,2,4096]{2,1,0:T(2,128)(2,1)} %w_out.1), custom_call_target="tpu_custom_call" | custom-call | tf_op jit(solution)/shard_map/pallas_call | solution.py:581
  115.9 1.9 %copy.9 = f32[256,512]{1,0:T(8,128)} copy(f32[256,512]{1,0:T(8,128)} %shard_map.64) | data formatting | bytes 1048576

commit v7 on v6

--- a/solution.py
+++ b/solution.py
@@ -537,13 +537,19 @@
 
     finish(1)
     result[...] = direct[:frame_count]
+    rest = pl.ds(window, frame_count - window)
+    done_rest = pltpu.make_async_copy(
+        result.at[rest], out.at[rest], local_sems.at[MAX_LOCAL - 2]
+    )
+    done_rest.start()
 
     @pl.when(jnp.logical_not(first))
     def _():
         carried.wait_recv()
         result[:window] += tail_in[...].astype(F32)
 
-    done = pltpu.make_async_copy(result, out, local_sems.at[MAX_LOCAL - 1])
+    top = pl.ds(0, window)
+    done = pltpu.make_async_copy(result.at[top], out.at[top], local_sems.at[MAX_LOCAL - 1])
     done.start()
     @pl.when(jnp.logical_not(final))
     def _():
@@ -563,6 +569,7 @@
             to_end[t].wait_send()
 
     done.wait()
+    done_rest.wait()
 
 
 def shards(frames, cotangent, w_qkv, w_out, starts, counts):

time: 118 us -> 118 us (level)
  no operation moved by 1% of the time
where the time goes in v7:
time: 118 us
  Pallas kernels  115 us (97%)
  local copies, waits for them, and re-layouts  1.87 us (2%)
    pallas_call x1, Pallas kernels, shards(): pl.pallas_call(kernel, out_shape=jax.ShapeDtypeStruct((frame_count, slab)...  115 us

profile of v7, /device:TPU:56, one launch (start us, length us, event | category | flops | bytes accessed | tf_op | source)
XLA Modules:
  0.0 117.7 jit_solution(11007101264105492805)
XLA Ops:
  0.7 115.1 %shard_map.64 = f32[256,512]{1,0:T(8,128)} custom-call(s32[3]{0:T(128)} %starts.1, s32[1]{0:T(128)S(6)} %copy.8.counts, bf16[256,512]{1,0:T(8,128)(2,1)} %frames.1, bf16[384,4096]{1,0:T(8,128)(2,1)} %bitcast.1, bf16[64,2,384]{2,1,0:T(2,128)(2,1)} %w_qkv.1, bf16[2,2,4096]{2,1,0:T(2,128)(2,1)} %w_out.1), custom_call_target="tpu_custom_call" | custom-call | tf_op jit(solution)/shard_map/pallas_call | solution.py:588
  115.8 1.9 %copy.9 = f32[256,512]{1,0:T(8,128)} copy(f32[256,512]{1,0:T(8,128)} %shard_map.64) | data formatting | bytes 1048576
